TPU v7x, 256 devices: a whole 4x4x8 slice. The times are simulated.
256 devices in a mesh: row: 16 (over y, z_hi), col: 16 (over x, z_lo, core).
Axes of the slice: x: 4, y: 4, z: 8 (z_hi: 4, z_lo: 2; z = z_hi * 2 + z_lo), core: 2. Of those that a mesh axis runs over, the one named last changes fastest.
Arguments:
- pair: bfloat16 [1024, 1024, 128], P('row', 'col'), may hold values from -6 to 6
- projection: bfloat16 [128, 640], replicated, may hold values from -0.5 to 0.5
- out_weight: bfloat16 [128, 128], replicated, may hold values from -0.5 to 0.5
Outputs:
- update: bfloat16 [1024, 1024, 128], P('row', 'col')
All inputs are finite; a program needn't handle non-finite values.
Results may differ from a plain program's by a relative error of at most 0.013.
Values may be sent and summed in bfloat16 or wider, within the bound.
A program may use at most 128 MiB of HBM per device.

v0:
```python
import jax
import jax.numpy as jnp
from jax import lax
from jax.sharding import PartitionSpec as P

epsilon = 1e-05


def layer_norm(values, axis):
    mean_value = jnp.mean(values, axis=axis, keepdims=True)
    centered = values - mean_value
    variance = jnp.mean(centered * centered, axis=axis, keepdims=True)
    return centered * lax.rsqrt(variance + epsilon)


def local(pair, projection, out_weight):
    row_count, col_count, channels = pair.shape
    hidden = out_weight.shape[0]
    normed = layer_norm(pair.astype(jnp.float32), -1).astype(jnp.bfloat16)
    projected = jnp.dot(
        normed.reshape(row_count * col_count, channels),
        projection,
        preferred_element_type=jnp.float32,
    )
    projected = projected.reshape(row_count, col_count, 4 * hidden + channels)
    left_side = (
        jax.nn.sigmoid(projected[..., :hidden]) * projected[..., hidden : 2 * hidden]
    ).astype(jnp.bfloat16)
    right_side = (
        jax.nn.sigmoid(projected[..., 2 * hidden : 3 * hidden])
        * projected[..., 3 * hidden : 4 * hidden]
    ).astype(jnp.bfloat16)
    gate_value = jax.nn.sigmoid(projected[..., 4 * hidden :])
    left_side = jnp.transpose(left_side, (2, 0, 1))
    right_side = jnp.transpose(right_side, (2, 0, 1))
    left_slab, right_slab = (
        lax.all_to_all(left_side, "col", split_axis=0, concat_axis=2, tiled=True),
        lax.all_to_all(right_side, "col", split_axis=0, concat_axis=2, tiled=True),
    )
    mixed_slab = jnp.einsum(
        "cik,cjk->cij",
        left_slab,
        lax.all_gather(right_slab, "row", axis=1, tiled=True),
        preferred_element_type=jnp.float32,
    ).astype(jnp.bfloat16)
    tile_values = lax.all_to_all(mixed_slab, "col", split_axis=2, concat_axis=0, tiled=True)
    normed_mix = layer_norm(tile_values.astype(jnp.float32), 0).astype(jnp.bfloat16)
    output = jnp.einsum("cij,cd->ijd", normed_mix, out_weight, preferred_element_type=jnp.float32)
    return (gate_value * output).astype(jnp.bfloat16)


def solution(mesh):
    placed = (P("row", "col", None), P(), P())
    return jax.shard_map(
        local, mesh=mesh, in_specs=placed, out_specs=P("row", "col", None), check_vma=False
    )
```

profile of v0, /device:TPU:1, one launch (start us, length us, event | category | flops | bytes accessed | tf_op | source)
XLA Modules:
  0.0 324.7 jit_solution(10569398139391638705)
XLA Ops:
  6.5 0.0 copy-start
  6.5 0.0 copy-start.3
  6.5 0.0 all-gather.2.cloned.1.call-start
  6.5 1.9 convert_reduce_fusion
  8.5 2.3 fusion.6
  10.9 0.0 copy-done
  10.9 0.0 copy-done.3
  10.9 1.8 fusion.25
  12.7 0.0 copy-start.2
  12.7 2.6 fusion.30
  15.3 1.7 copy-done.2
  17.0 3.9 %copy.15 = bf16[128,64,64]{2,1,0:T(8,128)(2,1)S(1)} copy(bf16[128,64,64]{0,2,1:T(8,128)(2,1)} %get-tuple-element.5) | data formatting | bytes 2097152 | tf_op jit(solution)/shard_map/transpose | solution.py:35
  21.0 2.2 reshape.41
  23.2 22.9 %all_to_all.45 = bf16[16,2,16384]{2,1,0:T(2,128)(2,1)} all-to-all(bf16[16,2,16384]{2,1,0:T(2,128)(2,1)} %reshape.41), channel_id=1, replica_groups=mesh['row'=16,'col'=16] {'col'}, dimensions={0} | all-to-all | bytes 2097152 | tf_op jit(solution)/shard_map/all_to_all | solution.py:38
  46.1 3.8 %reshape.42 = bf16[128,64,64]{2,1,0:T(8,128)(2,1)S(1)} reshape(bf16[16,2,16384]{2,1,0:T(2,128)(2,1)} %all_to_all.45) | data formatting | bytes 2097152
  49.9 2.8 copy.16
  52.6 4.1 %all_to_all.40 = bf16[8,64,1024]{2,1,0:T(8,128)(2,1)} reshape(bf16[8,64,16,64]{3,2,1,0:T(8,128)(2,1)} %copy.16) | data formatting | bytes 2097152 | tf_op jit(solution)/shard_map/all_to_all | solution.py:38
  56.7 0.0 all-gather.2.cloned.1.call-update
  56.8 3.0 copy.13
  59.8 1.5 reshape.39
  61.2 33.6 %all_to_all.46 = bf16[16,2,16384]{2,1,0:T(2,128)(2,1)} all-to-all(bf16[16,2,16384]{2,1,0:T(2,128)(2,1)S(1)} %reshape.39), channel_id=1, replica_groups=mesh['row'=16,'col'=16] {'col'}, dimensions={0} | all-to-all | bytes 2097152 | tf_op jit(solution)/shard_map/all_to_all | solution.py:37
  94.8 3.8 %reshape.40 = bf16[128,64,64]{2,1,0:T(8,128)(2,1)S(1)} reshape(bf16[16,2,16384]{2,1,0:T(2,128)(2,1)} %all_to_all.46) | data formatting | bytes 2097152
  98.6 2.7 copy.14
  101.3 3.2 all_to_all.36
  104.5 160.6 %all-gather.2.cloned.1.call-done = bf16[8,1024,1024]{2,1,0:T(8,128)(2,1)} async-done(((bf16[8,64,1024]{2,1,0:T(8,128)(2,1)}), bf16[8,1024,1024]{2,1,0:T(8,128)(2,1)}) %all-gather.2.cloned.1.call-update) | async-done | bytes 16777232 | tf_op jit(solution)/shard_map/all_gather | solution.py:43
  265.1 11.0 %convolution_convert_fusion = bf16[8,64,1024]{2,1,0:T(8,128)(2,1)S(1)} fusion(bf16[8,64,1024]{2,1,0:T(8,128)(2,1)S(1)} %all_to_all.36, bf16[8,1024,1024]{2,1,0:T(8,128)(2,1)} %all-gather.2.cloned.1.call-done), kind=kOutput, calls=%fused_computation.33 | convolution fusion | flops 1074266112 | bytes 18874368 | tf_op jit(solution)/shard_map/cik,cjk->cij/dot_general | solution.py:40
  276.1 1.7 copy.17
  277.8 1.5 reshape.43
  279.2 21.6 %all_to_all.47 = bf16[16,2,16384]{2,1,0:T(2,128)(2,1)} all-to-all(bf16[16,2,16384]{2,1,0:T(2,128)(2,1)S(1)} %reshape.43), channel_id=1, replica_groups=mesh['row'=16,'col'=16] {'col'}, dimensions={0} | all-to-all | bytes 2097152 | tf_op jit(solution)/shard_map/all_to_all | solution.py:46
  300.8 3.8 %reshape.44 = bf16[1024,8,64]{2,1,0:T(8,128)(2,1)S(1)} reshape(bf16[16,2,16384]{2,1,0:T(2,128)(2,1)} %all_to_all.47) | data formatting | bytes 2097152
  304.6 3.3 %copy.18 = f32[8,64,16,64]{3,1,0,2:T(8,128)} copy(bf16[8,64,16,64]{1,0,3,2:T(8,128)(2,1)S(1)} %bitcast.40) | data formatting | bytes 3145728 | tf_op jit(solution)/shard_map/convert_element_type | solution.py:47
  307.9 0.0 copy-start.1
  307.9 2.7 bitcast_reduce_fusion
  310.6 0.8 copy-done.1
  311.4 0.6 fusion.3
  312.0 0.0 copy-start.4
  312.0 0.7 fusion.1
  312.7 0.1 copy-done.4
  312.7 5.1 %fusion.22 = bf16[64,64,128]{2,1,0:T(8,128)(2,1)} fusion(f32[64,64,640]{2,1,0:T(8,128)} %copy-done.2, bf16[128,64,64]{2,1,0:T(8,128)(2,1)S(1)} %fusion.1, bf16[128,128]{1,0:T(8,128)(2,1)S(1)} %copy-done.4), kind=kOutput, calls=%fused_computation.32 | convolution fusion | flops 136839168 | bytes 4227072 | tf_op jit(solution)/shard_map/cij,cd->ijd/dot_general | solution.py:48
  (4 shorter events, 0.0 us)
Async XLA Ops:
  6.5 4.3 %copy-start = (bf16[128,640]{1,0:T(8,128)(2,1)S(1)}, bf16[128,640]{1,0:T(8,128)(2,1)}, u32[]{:S(2)}) copy-start(bf16[128,640]{1,0:T(8,128)(2,1)} %param.4) | copy-start | bytes 491524
  6.5 4.3 %copy-start.3 = (bf16[64,64,128]{2,1,0:T(8,128)(2,1)S(1)}, bf16[64,64,128]{2,1,0:T(8,128)(2,1)}, u32[]{:S(2)}) copy-start(bf16[64,64,128]{2,1,0:T(8,128)(2,1)} %param.3) | copy-start | bytes 3145732
  6.5 258.6 %all-gather.2.cloned.1.call-start = ((), (), s32[]{:S(2)}) async-start(), calls=%async_computation.3 | async-start | bytes 17825792 | tf_op jit(solution)/shard_map/all_gather | solution.py:43
  12.7 4.3 %copy-start.2 = (f32[64,64,640]{2,1,0:T(8,128)}, f32[64,64,640]{2,1,0:T(8,128)S(1)}, u32[]{:S(2)}) copy-start(f32[64,64,640]{2,1,0:T(8,128)S(1)} %fusion.25) | copy-start | bytes 31457284
  307.9 3.4 %copy-start.1 = (f32[8,64,16,64]{3,1,0,2:T(8,128)S(1)}, f32[8,64,16,64]{3,1,0,2:T(8,128)}, u32[]{:S(2)}) copy-start(f32[8,64,16,64]{3,1,0,2:T(8,128)} %copy.18) | copy-start | bytes 6291460
  312.0 0.8 copy-start.4
Sparse Core Ops, SparseCore 0:
  56.9 208.1 all-gather.1
where the time goes:
time: 325 us
  waiting for transfers between devices  161 us (50%)
  blocking collectives  78.1 us (24%)
  local copies, waits for them, and re-layouts  43.8 us (13%)
  matrix products  17.9 us (6%)
  between operations  13.5 us (4%)
  other arithmetic  10.8 us (3%)
    all_gather x1, waiting for transfers between devices, local(): lax.all_gather(right_slab, 'row', axis=1, tiled=True)  161 us
    all_to_all x1, blocking collectives, local(): lax.all_to_all(left_side, 'col', split_axis=0, concat_axis=2, tiled=True)  33.6 us
    all_to_all x1, blocking collectives, local(): lax.all_to_all(right_side, 'col', split_axis=0, concat_axis=2, tiled=True)  22.9 us
    all_to_all x1, blocking collectives, local(): lax.all_to_all(mixed_slab, 'col', split_axis=2, concat_axis=0, tiled=True)  21.6 us
    unnamed x16, local copies, waits for them, and re-layouts  19 us
    dot_general x1, matrix products, local(): jnp.einsum('cik,cjk->cij', left_slab, lax.all_gather(right_slab, 'row', a...  11 us
    all_to_all x2, local copies, waits for them, and re-layouts, local(): lax.all_to_all(right_side, 'col', split_axis=0, concat_axis=2, tiled=True)  6.87 us
  transfers between devices with their start and end apart: 1, of which 1 were waited for; matrix products, arithmetic and copies ran while one was open for 3% of the time, Pallas kernels for 0%

commit v1 on v0

v1 whole, which is shorter than its diff:
```python
import functools

import jax
import jax.numpy as jnp
from jax import lax
from jax.experimental import pallas as pl
from jax.experimental.pallas import tpu as pltpu
from jax.sharding import PartitionSpec as P

epsilon = 1e-05
MESH = pl.DeviceIdType.MESH
f32, bf16 = jnp.float32, jnp.bfloat16


def dot(a, b, dims):
    return lax.dot_general(a, b, (dims, ((), ())), preferred_element_type=f32)


def halves(first, second):
    return (
        jnp.concatenate([first[:, :64], second[:, :64]], axis=1),
        jnp.concatenate([first[:, 64:], second[:, 64:]], axis=1),
    )


def kernel(
    rows, cols, hidden,
    pair, projection, out_weight, update,
    right_f32, left_f32, normed, gate, weights, right_send, left_send, right_got, left_got,
    right_all, left_all, mixed, mixed_send, mixed_got, mixed_f32,
    send_sem, right_sem, left_sem, twin_sem, mixed_sem,
):
    chips = rows * cols // 2
    half_rows = rows // 2
    row, col = lax.axis_index("row"), lax.axis_index("col")
    core = lax.rem(col, 2)
    half = row // half_rows
    slot_row = lax.rem(row, half_rows)
    mine = row * (cols // 2) + col // 2
    twin = (row, col + 1 - 2 * core)

    barrier = pltpu.get_barrier_semaphore()

    def greet(step, _):
        other_row = lax.rem(row + step // cols, rows)
        other_col = lax.rem(col + lax.rem(step, cols), cols)
        pl.semaphore_signal(barrier, inc=1, device_id=(other_row, other_col), device_id_type=MESH)
        return 0

    lax.fori_loop(1, rows * cols, greet, 0)

    weights[...] = projection[:, : 4 * hidden].T

    def lines(step):
        block, inner = step // 8, lax.rem(step, 8) * 2
        return block * 32 + inner

    def norm_and_right(step, _):
        top = lines(step)
        values = jnp.concatenate(
            [pair[top], pair[top + 16], pair[top + 1], pair[top + 17]], axis=0
        ).astype(f32)
        centered = values - jnp.mean(values, axis=-1, keepdims=True)
        variance = jnp.mean(centered * centered, axis=-1, keepdims=True)
        unit = (centered * lax.rsqrt(variance + epsilon)).astype(bf16)
        normed[step] = unit
        both = dot(weights[2 * hidden : 4 * hidden], unit, ((1,), (1,)))
        side = jax.nn.sigmoid(both[:hidden]) * both[hidden:]
        right_f32[pl.ds(2 * step, hidden, stride=32), :] = side[:, :128]
        right_f32[pl.ds(2 * step + 1, hidden, stride=32), :] = side[:, 128:]
        return 0

    lax.fori_loop(0, 16, norm_and_right, 0)

    pl.semaphore_wait(barrier, rows * cols - 1)

    def target(step):
        other_row = lax.rem(row + step // (cols // 2), rows)
        other_pair = lax.rem(col // 2 + lax.rem(step, cols // 2), cols // 2)
        return other_row, other_pair, other_row * (cols // 2) + other_pair

    def send_side(held, outgoing, got, sem, sent, count, first, size):
        def one(step):
            other_row, other_pair, channel = target(step)
            base = pl.multiple_of(channel * 32 + first, 16)
            outgoing[channel, first : first + size] = held[pl.ds(base, size), :].astype(bf16)
            return outgoing.at[channel, pl.ds(first, size)], (other_row, other_pair * 2 + half)

        source, device = one(0)

        @pl.when(half == core)
        def _():
            pltpu.make_async_copy(source, got, sem).start()

        @pl.when(half != core)
        def _():
            pltpu.make_async_remote_copy(
                src_ref=source, dst_ref=got, send_sem=sent, recv_sem=sem, device_id=twin, device_id_type=MESH
            ).start()

        def body(step, _):
            source, device = one(step)
            pltpu.make_async_remote_copy(
                src_ref=source, dst_ref=got, send_sem=sent, recv_sem=sem, device_id=device, device_id_type=MESH
            ).start()
            return 0

        lax.fori_loop(1, chips, body, 0)

    send_side(right_f32, right_send, right_got.at[half, col, slot_row], right_sem, send_sem.at[0], chips, 0, 32)

    def left_side(step, _):
        both = dot(weights[: 2 * hidden], normed[step], ((1,), (1,)))
        side = jax.nn.sigmoid(both[:hidden]) * both[hidden:]
        left_f32[pl.ds(2 * step, hidden, stride=32), :] = side[:, :128]
        left_f32[pl.ds(2 * step + 1, hidden, stride=32), :] = side[:, 128:]
        return 0

    for part in range(2):
        lax.fori_loop(8 * part, 8 * part + 8, left_side, 0)
        send_side(
            left_f32, left_send, left_got.at[part, col, slot_row], left_sem.at[part], send_sem.at[1 + part],
            chips, 16 * part, 16,
        )

    def gate_of(step, _):
        gate[step] = jax.nn.sigmoid(dot(normed[step], projection[:, 4 * hidden :], ((1,), (0,))))
        return 0

    lax.fori_loop(0, 16, gate_of, 0)

    pltpu.make_async_copy(right_got.at[core], right_got.at[core], right_sem).wait()
    handed = pltpu.make_async_remote_copy(
        src_ref=right_got.at[core], dst_ref=right_got.at[core], send_sem=send_sem.at[3], recv_sem=twin_sem,
        device_id=twin, device_id_type=MESH,
    )
    handed.start()

    def arrange_right(which):
        def body(line, _):
            base = pl.multiple_of((which * half_rows + line) * 64, 64)
            for m in range(cols // 2):
                first, second = right_got[which, 2 * m, line], right_got[which, 2 * m + 1, line]
                low, high = halves(first, second)
                span = slice(128 * m, 128 * m + 128)
                right_all[pl.ds(base, 16), span] = low[:16]
                right_all[pl.ds(base + 16, 16), span] = high[:16]
                right_all[pl.ds(base + 32, 16), span] = low[16:]
                right_all[pl.ds(base + 48, 16), span] = high[16:]
            return 0

        lax.fori_loop(0, half_rows, body, 0)

    arrange_right(core)
    handed.wait_recv()
    arrange_right(1 - core)

    for part in range(2):
        pltpu.make_async_copy(left_got.at[part], left_got.at[part], left_sem.at[part]).wait()

        def arrange_left(line, _):
            base = pl.multiple_of(line * 32, 32)
            for m in range(cols // 2):
                low, high = halves(left_got[part, 2 * m, line], left_got[part, 2 * m + 1, line])
                left_all[pl.ds(base, 16), 128 * m : 128 * m + 128] = low
                left_all[pl.ds(base + 16, 16), 128 * m : 128 * m + 128] = high
            return 0

        lax.fori_loop(0, half_rows, arrange_left, 0)

        def multiply(step, _):
            base = pl.multiple_of(step * 256, 256)
            mixed[...] = dot(left_all[...], right_all[pl.ds(base, 256), :], ((1,), (1,))).astype(bf16)
            for line in range(half_rows):
                for m in range(2):
                    span = slice(128 * m, 128 * m + 128)
                    low, high = halves(mixed[line * 32 : line * 32 + 16, span], mixed[line * 32 + 16 : line * 32 + 32, span])
                    mixed_send[part, line, step * 4 + 2 * m] = low
                    mixed_send[part, line, step * 4 + 2 * m + 1] = high
            return 0

        lax.fori_loop(0, cols // 4, multiply, 0)

        got = mixed_got.at[part, mine]

        def send_mixed(step, _):
            line = lax.rem(slot_row + step // cols, half_rows)
            other = lax.rem(col + lax.rem(step, cols), cols)
            source = mixed_send.at[part, line, other]
            own = jnp.logical_and(step == 0, half == core)

            @pl.when(own)
            def _():
                pltpu.make_async_copy(source, got, mixed_sem.at[part]).start()

            @pl.when(jnp.logical_not(own))
            def _():
                pltpu.make_async_remote_copy(
                    src_ref=source, dst_ref=got, send_sem=send_sem.at[4 + part], recv_sem=mixed_sem.at[part],
                    device_id=(core * half_rows + line, other), device_id_type=MESH,
                ).start()

            return 0

        lax.fori_loop(0, half_rows * cols, send_mixed, 0)

    for part in range(2):
        pltpu.make_async_copy(mixed_got.at[part], mixed_got.at[part], mixed_sem.at[part]).wait()

        total = jnp.zeros((16, 128), f32)
        total = lax.fori_loop(0, hidden, lambda c, t: t + mixed_got[part, c].astype(f32), total)
        mean = total * (1.0 / hidden)

        def square(c, t):
            centered = mixed_got[part, c].astype(f32) - mean
            return t + centered * centered

        scale = lax.rsqrt(lax.fori_loop(0, hidden, square, jnp.zeros((16, 128), f32)) * (1.0 / hidden) + epsilon)

        def norm(c, _):
            mixed_f32[pl.ds(pl.multiple_of(c * 16, 16), 16), :] = (mixed_got[part, c].astype(f32) - mean) * scale
            return 0

        lax.fori_loop(0, hidden, norm, 0)

        def finish(line, _):
            unit = mixed_f32[pl.ds(line, hidden, stride=16), :].astype(bf16)
            product = dot(unit, out_weight[...], ((0,), (0,)))
            step = part * 8 + line // 2
            result = (gate[step, pl.ds(pl.multiple_of(lax.rem(line, 2) * 128, 128), 128), :] * product).astype(bf16)
            update[part * 32 + line] = result[:64]
            update[part * 32 + line + 16] = result[64:]
            return 0

        lax.fori_loop(0, 16, finish, 0)

    sent_bytes = chips - 1 + jnp.where(half == core, 0, 1)

    @pl.when(half == core)
    def _():
        pltpu.make_async_copy(right_send.at[pl.ds(0, chips - 1)], right_send.at[pl.ds(0, chips - 1)], send_sem.at[0]).wait()
        for part in range(2):
            span = left_send.at[pl.ds(0, chips - 1), pl.ds(0, 16)]
            pltpu.make_async_copy(span, span, send_sem.at[1 + part]).wait()
            span = mixed_got.at[0, pl.ds(0, chips - 1)]
            pltpu.make_async_copy(span, span, send_sem.at[4 + part]).wait()

    @pl.when(half != core)
    def _():
        pltpu.make_async_copy(right_send, right_send, send_sem.at[0]).wait()
        for part in range(2):
            span = left_send.at[:, pl.ds(0, 16)]
            pltpu.make_async_copy(span, span, send_sem.at[1 + part]).wait()
            span = mixed_got.at[0]
            pltpu.make_async_copy(span, span, send_sem.at[4 + part]).wait()

    handed.wait_send()


def local(rows, cols, pair, projection, out_weight):
    hidden = out_weight.shape[0]
    half_rows = rows // 2
    vmem = pl.BlockSpec(memory_space=pltpu.VMEM)
    length = cols * 64
    return pl.pallas_call(
        functools.partial(kernel, rows, cols, hidden),
        out_shape=jax.ShapeDtypeStruct(pair.shape, bf16),
        in_specs=[vmem] * 3,
        out_specs=vmem,
        scratch_shapes=[
            pltpu.VMEM((hidden * 32, 128), f32),
            pltpu.VMEM((hidden * 32, 128), f32),
            pltpu.VMEM((16, 256, 128), bf16),
            pltpu.VMEM((16, 256, 128), f32),
            pltpu.VMEM((4 * hidden, 128), bf16),
            pltpu.VMEM((hidden, 32, 128), bf16),
            pltpu.VMEM((hidden, 32, 128), bf16),
            pltpu.VMEM((2, cols, half_rows, 32, 128), bf16),
            pltpu.VMEM((2, cols, half_rows, 16, 128), bf16),
            pltpu.VMEM((rows * 64, length), bf16),
            pltpu.VMEM((half_rows * 32, length), bf16),
            pltpu.VMEM((half_rows * 32, 256), bf16),
            pltpu.VMEM((2, half_rows, cols, 16, 128), bf16),
            pltpu.VMEM((2, hidden, 16, 128), bf16),
            pltpu.VMEM((hidden * 16, 128), f32),
            pltpu.SemaphoreType.DMA((6,)),
            pltpu.SemaphoreType.DMA,
            pltpu.SemaphoreType.DMA((2,)),
            pltpu.SemaphoreType.DMA,
            pltpu.SemaphoreType.DMA((2,)),
        ],
        compiler_params=pltpu.CompilerParams(
            collective_id=0, has_side_effects=True, vmem_limit_bytes=48 * 2**20
        ),
        name="triangle",
    )(pair, projection, out_weight)


def solution(mesh):
    placed = (P("row", "col", None), P(), P())
    rows, cols = mesh.shape["row"], mesh.shape["col"]
    return jax.shard_map(
        functools.partial(local, rows, cols),
        mesh=mesh,
        in_specs=placed,
        out_specs=P("row", "col", None),
        check_vma=False,
    )
```

time: 325 us -> 103 us (0.32)
  waiting for transfers between devices: 161 us -> 0 us
  Pallas kernels: 0 us -> 99.3 us
  blocking collectives: 78.1 us -> 0 us
  local copies, waits for them, and re-layouts: 43.8 us -> 3.87 us
  matrix products: 17.9 us -> 0 us
  between operations: 13.5 us -> 0.01 us
  other arithmetic: 10.8 us -> 0 us
    all_gather x1 -> x0, waiting for transfers between devices: 161 us -> none  [local(): lax.all_gather(right_slab, 'row', axis=1, tiled=True)]
    pallas_call x0 -> x1, Pallas kernels: none -> 99.3 us  [local(): pl.pallas_call(functools.partial(kernel, rows, cols, hidden), out_shape=j...]
    all_to_all x3 -> x0, blocking collectives: 78.1 us -> none  [the longest x1 33.6 us: local(): lax.all_to_all(left_side, 'col', split_axis=0, concat_axis=2, tiled=True)]
    dot_general x3 -> x0, matrix products: 17.9 us -> none  [the longest x1 11 us: local(): jnp.einsum('cik,cjk->cij', left_slab, lax.all_gather(right_slab, 'row', a...]
    unnamed x16 -> x7, local copies, waits for them, and re-layouts: 19 us -> 3.87 us
    all_to_all x4 -> x0, local copies, waits for them, and re-layouts: 12.8 us -> none  [the longest x2 6.87 us: local(): lax.all_to_all(right_side, 'col', split_axis=0, concat_axis=2, tiled=True)]
    reduce_sum x4 -> x0, other arithmetic: 7.55 us -> none  [the longest x2 4.61 us: layer_norm(): mean_value = jnp.mean(values, axis=axis, keepdims=True)]
    transpose x2 -> x0, local copies, waits for them, and re-layouts: 6.92 us -> none  [the longest x1 3.93 us: local(): right_side = jnp.transpose(right_side, (2, 0, 1))]
  transfers between devices with their start and end apart: 1 -> 0, of which waited for: 1 -> 0; matrix products, arithmetic and copies ran while one was open for 3% -> 0% of each run, Pallas kernels for 0% -> 0%
where the time goes in v1:
time: 103 us
  Pallas kernels  99.3 us (96%)
  local copies, waits for them, and re-layouts  3.87 us (4%)
    pallas_call x1, Pallas kernels, local(): pl.pallas_call(functools.partial(kernel, rows, cols, hidden), out_shape=j...  99.3 us
    unnamed x7, local copies, waits for them, and re-layouts  3.87 us

profile of v1, /device:TPU:1, one launch (start us, length us, event | category | flops | bytes accessed | tf_op | source)
XLA Modules:
  0.0 103.2 jit_solution(13366993231884698)
XLA Ops:
  0.0 0.0 copy-start
  0.0 1.2 %copy-done = bf16[64,64,128]{2,1,0:T(8,128)(2,1)S(1)} copy-done((bf16[64,64,128]{2,1,0:T(8,128)(2,1)S(1)}, bf16[64,64,128]{2,1,0:T(8,128)(2,1)}, u32[]{:S(2)}) %copy-start) | copy-done | bytes 1048600
  1.2 0.0 copy-start.1
  1.2 0.9 copy-done.1
  2.1 0.0 copy-start.2
  2.1 0.8 copy-done.2
  2.9 99.3 %triangle.1 = bf16[64,64,128]{2,1,0:T(8,128)(2,1)S(1)} custom-call(bf16[64,64,128]{2,1,0:T(8,128)(2,1)S(1)} %copy-done, bf16[128,640]{1,0:T(8,128)(2,1)S(1)} %copy-done.1, bf16[128,128]{1,0:T(8,128)(2,1)S(1)} %copy-done.2), custom_call_target="tpu_custom_call" | custom-call | tf_op jit(solution)/shard_map/triangle/pallas_call | solution.py:265
  102.2 1.0 copy.5
Async XLA Ops:
  0.0 1.2 %copy-start = (bf16[64,64,128]{2,1,0:T(8,128)(2,1)S(1)}, bf16[64,64,128]{2,1,0:T(8,128)(2,1)}, u32[]{:S(2)}) copy-start(bf16[64,64,128]{2,1,0:T(8,128)(2,1)} %pair.1) | copy-start | bytes 3145732
  1.2 0.9 copy-start.1
  2.1 0.8 copy-start.2

commit v2 on v1

--- a/solution.py
+++ b/solution.py
@@ -25,10 +25,10 @@
 
 def kernel(
     rows, cols, hidden,
-    pair, projection, out_weight, update,
-    right_f32, left_f32, normed, gate, weights, right_send, left_send, right_got, left_got,
+    pair_hbm, projection_hbm, out_weight_hbm, update,
+    pair, projection, out_weight, right_f32, left_f32, normed, gate, weights, right_send, left_send, right_got, left_got,
     right_all, left_all, mixed, mixed_send, mixed_got, mixed_f32,
-    send_sem, right_sem, left_sem, twin_sem, mixed_sem,
+    load_sem, entered_sem, send_sem, right_sem, left_sem, twin_sem, mixed_sem,
 ):
     chips = rows * cols // 2
     half_rows = rows // 2
@@ -39,23 +39,29 @@
     mine = row * (cols // 2) + col // 2
     twin = (row, col + 1 - 2 * core)
 
+    loads = [
+        pltpu.make_async_copy(projection_hbm, projection, load_sem.at[0]),
+        pltpu.make_async_copy(pair_hbm.at[pl.ds(0, 32)], pair.at[pl.ds(0, 32)], load_sem.at[1]),
+        pltpu.make_async_copy(pair_hbm.at[pl.ds(32, 32)], pair.at[pl.ds(32, 32)], load_sem.at[2]),
+        pltpu.make_async_copy(out_weight_hbm, out_weight, load_sem.at[3]),
+    ]
+    for load in loads:
+        load.start()
+
     barrier = pltpu.get_barrier_semaphore()
-
-    def greet(step, _):
-        other_row = lax.rem(row + step // cols, rows)
-        other_col = lax.rem(col + lax.rem(step, cols), cols)
-        pl.semaphore_signal(barrier, inc=1, device_id=(other_row, other_col), device_id_type=MESH)
-        return 0
-
-    lax.fori_loop(1, rows * cols, greet, 0)
-
+    row_peers = [(lax.rem(row + step, rows), col) for step in range(1, rows)]
+    col_peers = [(row, lax.rem(col + step, cols)) for step in range(1, cols)]
+    for peer in row_peers + col_peers:
+        pl.semaphore_signal(barrier, inc=1, device_id=peer, device_id_type=MESH)
+
+    loads[0].wait()
     weights[...] = projection[:, : 4 * hidden].T
 
     def lines(step):
         block, inner = step // 8, lax.rem(step, 8) * 2
         return block * 32 + inner
 
-    def norm_and_right(step, _):
+    def norm(step, _):
         top = lines(step)
         values = jnp.concatenate(
             [pair[top], pair[top + 16], pair[top + 1], pair[top + 17]], axis=0
@@ -64,22 +70,31 @@
         variance = jnp.mean(centered * centered, axis=-1, keepdims=True)
         unit = (centered * lax.rsqrt(variance + epsilon)).astype(bf16)
         normed[step] = unit
-        both = dot(weights[2 * hidden : 4 * hidden], unit, ((1,), (1,)))
+        return 0
+
+    def right_side(step, _):
+        both = dot(weights[2 * hidden : 4 * hidden], normed[step], ((1,), (1,)))
         side = jax.nn.sigmoid(both[:hidden]) * both[hidden:]
         right_f32[pl.ds(2 * step, hidden, stride=32), :] = side[:, :128]
         right_f32[pl.ds(2 * step + 1, hidden, stride=32), :] = side[:, 128:]
         return 0
 
-    lax.fori_loop(0, 16, norm_and_right, 0)
-
-    pl.semaphore_wait(barrier, rows * cols - 1)
+    loads[1].wait()
+    lax.fori_loop(0, 8, norm, 0, unroll=2)
+    pl.semaphore_wait(barrier, rows - 1 + cols - 1)
+    for peer in row_peers:
+        pl.semaphore_signal(entered_sem, inc=1, device_id=peer, device_id_type=MESH)
+    loads[2].wait()
+    lax.fori_loop(8, 16, norm, 0, unroll=2)
+    lax.fori_loop(0, 16, right_side, 0, unroll=4)
+    pl.semaphore_wait(entered_sem, rows - 1)
 
     def target(step):
         other_row = lax.rem(row + step // (cols // 2), rows)
         other_pair = lax.rem(col // 2 + lax.rem(step, cols // 2), cols // 2)
         return other_row, other_pair, other_row * (cols // 2) + other_pair
 
-    def send_side(held, outgoing, got, sem, sent, count, first, size):
+    def send_side(held, outgoing, got, sem, sent, first, size):
         def one(step):
             other_row, other_pair, channel = target(step)
             base = pl.multiple_of(channel * 32 + first, 16)
@@ -105,9 +120,12 @@
             ).start()
             return 0
 
-        lax.fori_loop(1, chips, body, 0)
-
-    send_side(right_f32, right_send, right_got.at[half, col, slot_row], right_sem, send_sem.at[0], chips, 0, 32)
+        body(1, 0)
+        body(2, 0)
+        body(3, 0)
+        lax.fori_loop(4, chips, body, 0, unroll=4)
+
+    send_side(right_f32, right_send, right_got.at[half, col, slot_row], right_sem, send_sem.at[0], 0, 32)
 
     def left_side(step, _):
         both = dot(weights[: 2 * hidden], normed[step], ((1,), (1,)))
@@ -117,17 +135,17 @@
         return 0
 
     for part in range(2):
-        lax.fori_loop(8 * part, 8 * part + 8, left_side, 0)
+        lax.fori_loop(8 * part, 8 * part + 8, left_side, 0, unroll=4)
         send_side(
             left_f32, left_send, left_got.at[part, col, slot_row], left_sem.at[part], send_sem.at[1 + part],
-            chips, 16 * part, 16,
+            16 * part, 16,
         )
 
     def gate_of(step, _):
         gate[step] = jax.nn.sigmoid(dot(normed[step], projection[:, 4 * hidden :], ((1,), (0,))))
         return 0
 
-    lax.fori_loop(0, 16, gate_of, 0)
+    lax.fori_loop(0, 16, gate_of, 0, unroll=4)
 
     pltpu.make_async_copy(right_got.at[core], right_got.at[core], right_sem).wait()
     handed = pltpu.make_async_remote_copy(
@@ -202,26 +220,27 @@
 
             return 0
 
-        lax.fori_loop(0, half_rows * cols, send_mixed, 0)
-
+        lax.fori_loop(0, half_rows * cols, send_mixed, 0, unroll=4)
+
+    loads[3].wait()
     for part in range(2):
         pltpu.make_async_copy(mixed_got.at[part], mixed_got.at[part], mixed_sem.at[part]).wait()
 
         total = jnp.zeros((16, 128), f32)
-        total = lax.fori_loop(0, hidden, lambda c, t: t + mixed_got[part, c].astype(f32), total)
+        total = lax.fori_loop(0, hidden, lambda c, t: t + mixed_got[part, c].astype(f32), total, unroll=min(16, hidden))
         mean = total * (1.0 / hidden)
 
         def square(c, t):
             centered = mixed_got[part, c].astype(f32) - mean
             return t + centered * centered
 
-        scale = lax.rsqrt(lax.fori_loop(0, hidden, square, jnp.zeros((16, 128), f32)) * (1.0 / hidden) + epsilon)
-
-        def norm(c, _):
+        scale = lax.rsqrt(lax.fori_loop(0, hidden, square, jnp.zeros((16, 128), f32), unroll=min(16, hidden)) * (1.0 / hidden) + epsilon)
+
+        def scaled(c, _):
             mixed_f32[pl.ds(pl.multiple_of(c * 16, 16), 16), :] = (mixed_got[part, c].astype(f32) - mean) * scale
             return 0
 
-        lax.fori_loop(0, hidden, norm, 0)
+        lax.fori_loop(0, hidden, scaled, 0, unroll=min(16, hidden))
 
         def finish(line, _):
             unit = mixed_f32[pl.ds(line, hidden, stride=16), :].astype(bf16)
@@ -232,9 +251,7 @@
             update[part * 32 + line + 16] = result[64:]
             return 0
 
-        lax.fori_loop(0, 16, finish, 0)
-
-    sent_bytes = chips - 1 + jnp.where(half == core, 0, 1)
+        lax.fori_loop(0, 16, finish, 0, unroll=8)
 
     @pl.when(half == core)
     def _():
@@ -265,9 +282,12 @@
     return pl.pallas_call(
         functools.partial(kernel, rows, cols, hidden),
         out_shape=jax.ShapeDtypeStruct(pair.shape, bf16),
-        in_specs=[vmem] * 3,
+        in_specs=[pl.BlockSpec(memory_space=pltpu.HBM)] * 3,
         out_specs=vmem,
         scratch_shapes=[
+            pltpu.VMEM(pair.shape, bf16),
+            pltpu.VMEM(projection.shape, bf16),
+            pltpu.VMEM(out_weight.shape, bf16),
             pltpu.VMEM((hidden * 32, 128), f32),
             pltpu.VMEM((hidden * 32, 128), f32),
             pltpu.VMEM((16, 256, 128), bf16),
@@ -283,6 +303,8 @@
             pltpu.VMEM((2, half_rows, cols, 16, 128), bf16),
             pltpu.VMEM((2, hidden, 16, 128), bf16),
             pltpu.VMEM((hidden * 16, 128), f32),
+            pltpu.SemaphoreType.DMA((4,)),
+            pltpu.SemaphoreType.REGULAR,
             pltpu.SemaphoreType.DMA((6,)),
             pltpu.SemaphoreType.DMA,
             pltpu.SemaphoreType.DMA((2,)),

time: 103 us -> 94.3 us (0.916)
  Pallas kernels: 99.3 us -> 90.2 us
    pallas_call x1, Pallas kernels: 99.3 us -> 90.2 us  [local(): pl.pallas_call(functools.partial(kernel, rows, cols, hidden), out_shape=j...]
where the time goes in v2:
time: 94.3 us; the launch traced here: 94.1 us
  Pallas kernels  90.2 us (96%)
  local copies, waits for them, and re-layouts  3.87 us (4%)
    pallas_call x1, Pallas kernels, local(): pl.pallas_call(functools.partial(kernel, rows, cols, hidden), out_shape=j...  90.2 us
    unnamed x7, local copies, waits for them, and re-layouts  3.87 us

profile of v2, /device:TPU:1, one launch (start us, length us, event | category | flops | bytes accessed | tf_op | source)
XLA Modules:
  0.0 94.1 jit_solution(8992627471075701299)
XLA Ops:
  0.0 0.0 copy-start
  0.0 1.2 %copy-done = bf16[64,64,128]{2,1,0:T(8,128)(2,1)S(1)} copy-done((bf16[64,64,128]{2,1,0:T(8,128)(2,1)S(1)}, bf16[64,64,128]{2,1,0:T(8,128)(2,1)}, u32[]{:S(2)}) %copy-start) | copy-done | bytes 1048600
  1.2 0.0 copy-start.1
  1.2 0.9 copy-done.1
  2.1 0.0 copy-start.2
  2.1 0.8 copy-done.2
  2.9 90.2 %triangle.1 = bf16[64,64,128]{2,1,0:T(8,128)(2,1)S(1)} custom-call(bf16[64,64,128]{2,1,0:T(8,128)(2,1)S(1)} %copy-done, bf16[128,640]{1,0:T(8,128)(2,1)S(1)} %copy-done.1, bf16[128,128]{1,0:T(8,128)(2,1)S(1)} %copy-done.2), custom_call_target="tpu_custom_call" | custom-call | tf_op jit(solution)/shard_map/triangle/pallas_call | solution.py:282
  93.2 1.0 %copy.5 = bf16[64,64,128]{2,1,0:T(8,128)(2,1)} copy(bf16[64,64,128]{2,1,0:T(8,128)(2,1)S(1)} %triangle.1) | data formatting | bytes 2097152
Async XLA Ops:
  0.0 1.2 %copy-start = (bf16[64,64,128]{2,1,0:T(8,128)(2,1)S(1)}, bf16[64,64,128]{2,1,0:T(8,128)(2,1)}, u32[]{:S(2)}) copy-start(bf16[64,64,128]{2,1,0:T(8,128)(2,1)} %pair_hbm.1) | copy-start | bytes 3145732
  1.2 0.9 copy-start.1
  2.1 0.8 copy-start.2

commit v3 on v2

--- a/solution.py
+++ b/solution.py
@@ -16,6 +16,10 @@
     return lax.dot_general(a, b, (dims, ((), ())), preferred_element_type=f32)
 
 
+def rem(a, b):
+    return a % b if isinstance(a, int) else lax.rem(a, b)
+
+
 def halves(first, second):
     return (
         jnp.concatenate([first[:, :64], second[:, :64]], axis=1),
@@ -25,19 +29,27 @@
 
 def kernel(
     rows, cols, hidden,
-    pair_hbm, projection_hbm, out_weight_hbm, update,
-    pair, projection, out_weight, right_f32, left_f32, normed, gate, weights, right_send, left_send, right_got, left_got,
+    pair_hbm, projection_hbm, out_weight_hbm, update_hbm,
+    pair, projection, out_weight, update, right_f32, left_f32, normed, gate, weights, right_send, left_send, right_got, left_got,
     right_all, left_all, mixed, mixed_send, mixed_got, mixed_f32,
-    load_sem, entered_sem, send_sem, right_sem, left_sem, twin_sem, mixed_sem,
+    load_sem, store_sem, entered_sem, send_sem, right_sem, left_sem, twin_sem, mixed_sem,
 ):
     chips = rows * cols // 2
     half_rows = rows // 2
     row, col = lax.axis_index("row"), lax.axis_index("col")
-    core = lax.rem(col, 2)
+    planes, lines_z = rows // 4, 8
+    columns = cols // 4
+    x, y, z, core = col // 4, row // 4, rem(row, 4) * 2 + rem(col // 2, 2), rem(col, 2)
     half = row // half_rows
-    slot_row = lax.rem(row, half_rows)
+    slot_row = rem(row, half_rows)
     mine = row * (cols // 2) + col // 2
     twin = (row, col + 1 - 2 * core)
+
+    def chip(x, y, z):
+        return y * 4 + z // 2, x * 2 + rem(z, 2)
+
+    def along_z(k):
+        return rem(z + 4 + ((k + 1) // 2) * (1 - 2 * rem(k, 2)) + lines_z, lines_z)
 
     loads = [
         pltpu.make_async_copy(projection_hbm, projection, load_sem.at[0]),
@@ -49,16 +61,21 @@
         load.start()
 
     barrier = pltpu.get_barrier_semaphore()
-    row_peers = [(lax.rem(row + step, rows), col) for step in range(1, rows)]
-    col_peers = [(row, lax.rem(col + step, cols)) for step in range(1, cols)]
-    for peer in row_peers + col_peers:
+    x_peers = [(row, rem(col + 4 * step, cols)) for step in range(1, columns)]
+    for k in range(lines_z):
+        for step in range(planes):
+            place, pair_place = chip(x, rem(y + step, planes), along_z(k))
+            if k < lines_z - 1 or step > 0:
+                pl.semaphore_signal(barrier, inc=1, device_id=(place, pair_place * 2), device_id_type=MESH)
+                pl.semaphore_signal(barrier, inc=1, device_id=(place, pair_place * 2 + 1), device_id_type=MESH)
+    for peer in [twin] + x_peers:
         pl.semaphore_signal(barrier, inc=1, device_id=peer, device_id_type=MESH)
 
     loads[0].wait()
     weights[...] = projection[:, : 4 * hidden].T
 
     def lines(step):
-        block, inner = step // 8, lax.rem(step, 8) * 2
+        block, inner = step // 8, rem(step, 8) * 2
         return block * 32 + inner
 
     def norm(step, _):
@@ -79,53 +96,58 @@
         right_f32[pl.ds(2 * step + 1, hidden, stride=32), :] = side[:, 128:]
         return 0
 
-    loads[1].wait()
-    lax.fori_loop(0, 8, norm, 0, unroll=2)
-    pl.semaphore_wait(barrier, rows - 1 + cols - 1)
-    for peer in row_peers:
-        pl.semaphore_signal(entered_sem, inc=1, device_id=peer, device_id_type=MESH)
-    loads[2].wait()
-    lax.fori_loop(8, 16, norm, 0, unroll=2)
+    for part in range(2):
+        loads[1 + part].wait()
+        lax.fori_loop(8 * part, 8 * part + 8, norm, 0, unroll=2)
     lax.fori_loop(0, 16, right_side, 0, unroll=4)
-    pl.semaphore_wait(entered_sem, rows - 1)
-
-    def target(step):
-        other_row = lax.rem(row + step // (cols // 2), rows)
-        other_pair = lax.rem(col // 2 + lax.rem(step, cols // 2), cols // 2)
-        return other_row, other_pair, other_row * (cols // 2) + other_pair
-
-    def send_side(held, outgoing, got, sem, sent, first, size):
-        def one(step):
-            other_row, other_pair, channel = target(step)
+
+    def send_side(held, outgoing, got, sem, sent, first, size, start, stop):
+        def fill(channel):
             base = pl.multiple_of(channel * 32 + first, 16)
             outgoing[channel, first : first + size] = held[pl.ds(base, size), :].astype(bf16)
-            return outgoing.at[channel, pl.ds(first, size)], (other_row, other_pair * 2 + half)
-
-        source, device = one(0)
-
-        @pl.when(half == core)
-        def _():
-            pltpu.make_async_copy(source, got, sem).start()
-
-        @pl.when(half != core)
-        def _():
+            return outgoing.at[channel, pl.ds(first, size)]
+
+        def body(step, _):
+            place, pair_place = chip(
+                rem(x + step // (planes * lines_z), columns),
+                rem(y + step // lines_z + 1, planes),
+                along_z(rem(step, lines_z)),
+            )
             pltpu.make_async_remote_copy(
-                src_ref=source, dst_ref=got, send_sem=sent, recv_sem=sem, device_id=twin, device_id_type=MESH
+                src_ref=fill(place * (cols // 2) + pair_place), dst_ref=got, send_sem=sent, recv_sem=sem,
+                device_id=(place, pair_place * 2 + half), device_id_type=MESH,
             ).start()
-
-        def body(step, _):
-            source, device = one(step)
-            pltpu.make_async_remote_copy(
-                src_ref=source, dst_ref=got, send_sem=sent, recv_sem=sem, device_id=device, device_id_type=MESH
-            ).start()
-            return 0
-
-        body(1, 0)
-        body(2, 0)
-        body(3, 0)
-        lax.fori_loop(4, chips, body, 0, unroll=4)
-
-    send_side(right_f32, right_send, right_got.at[half, col, slot_row], right_sem, send_sem.at[0], 0, 32)
+            return 0
+
+        own = planes * lines_z - 1
+        if start <= own:
+            head = (own - start) % 4
+            for step in range(start, start + head):
+                body(step, 0)
+            lax.fori_loop(start + head, own, body, 0, unroll=4)
+            source = fill(mine)
+
+            @pl.when(half == core)
+            def _():
+                pltpu.make_async_copy(source, got, sem).start()
+
+            @pl.when(half != core)
+            def _():
+                pltpu.make_async_remote_copy(
+                    src_ref=source, dst_ref=got, send_sem=sent, recv_sem=sem, device_id=twin, device_id_type=MESH
+                ).start()
+
+            start = own + 1
+        lax.fori_loop(start, stop, body, 0, unroll=4)
+
+    right_slot = right_got.at[half, col, slot_row]
+    near = planes * lines_z
+    pl.semaphore_wait(barrier, 2 * near - 1 + columns - 1)
+    for peer in x_peers:
+        pl.semaphore_signal(entered_sem, inc=1, device_id=peer, device_id_type=MESH)
+    send_side(right_f32, right_send, right_slot, right_sem, send_sem.at[0], 0, 32, 0, near)
+    pl.semaphore_wait(entered_sem, columns - 1)
+    send_side(right_f32, right_send, right_slot, right_sem, send_sem.at[0], 0, 32, near, chips)
 
     def left_side(step, _):
         both = dot(weights[: 2 * hidden], normed[step], ((1,), (1,)))
@@ -138,7 +160,7 @@
         lax.fori_loop(8 * part, 8 * part + 8, left_side, 0, unroll=4)
         send_side(
             left_f32, left_send, left_got.at[part, col, slot_row], left_sem.at[part], send_sem.at[1 + part],
-            16 * part, 16,
+            16 * part, 16, 0, chips,
         )
 
     def gate_of(step, _):
@@ -201,28 +223,39 @@
 
         got = mixed_got.at[part, mine]
 
+        def mixed_message(place, other):
+            line = rem(place, half_rows)
+            return pltpu.make_async_remote_copy(
+                src_ref=mixed_send.at[part, line, other], dst_ref=got,
+                send_sem=send_sem.at[4 + part], recv_sem=mixed_sem.at[part],
+                device_id=(place, other), device_id_type=MESH,
+            )
+
         def send_mixed(step, _):
-            line = lax.rem(slot_row + step // cols, half_rows)
-            other = lax.rem(col + lax.rem(step, cols), cols)
-            source = mixed_send.at[part, line, other]
-            own = jnp.logical_and(step == 0, half == core)
-
-            @pl.when(own)
-            def _():
-                pltpu.make_async_copy(source, got, mixed_sem.at[part]).start()
-
-            @pl.when(jnp.logical_not(own))
-            def _():
-                pltpu.make_async_remote_copy(
-                    src_ref=source, dst_ref=got, send_sem=send_sem.at[4 + part], recv_sem=mixed_sem.at[part],
-                    device_id=(core * half_rows + line, other), device_id_type=MESH,
-                ).start()
-
-            return 0
-
-        lax.fori_loop(0, half_rows * cols, send_mixed, 0, unroll=4)
+            k = rem(step, lines_z)
+            other_core = rem(core + 1 + step // lines_z, 2)
+            other_y = core * (planes // 2) + rem(y + 1 + step // (2 * lines_z), planes // 2)
+            other_x = rem(x + 1 + step // (planes * lines_z), columns)
+            place, pair_place = chip(other_x, other_y, along_z(k))
+            mixed_message(place, pair_place * 2 + other_core).start()
+            return 0
+
+        last = chips - 1
+        for step in range(3):
+            send_mixed(step, 0)
+        lax.fori_loop(3, last, send_mixed, 0, unroll=4)
+        place = core * half_rows + slot_row
+
+        @pl.when(half == core)
+        def _():
+            pltpu.make_async_copy(mixed_send.at[part, slot_row, col], got, mixed_sem.at[part]).start()
+
+        @pl.when(half != core)
+        def _():
+            mixed_message(place, col).start()
 
     loads[3].wait()
+    stores = []
     for part in range(2):
         pltpu.make_async_copy(mixed_got.at[part], mixed_got.at[part], mixed_sem.at[part]).wait()
 
@@ -246,12 +279,17 @@
             unit = mixed_f32[pl.ds(line, hidden, stride=16), :].astype(bf16)
             product = dot(unit, out_weight[...], ((0,), (0,)))
             step = part * 8 + line // 2
-            result = (gate[step, pl.ds(pl.multiple_of(lax.rem(line, 2) * 128, 128), 128), :] * product).astype(bf16)
+            result = (gate[step, pl.ds(pl.multiple_of(rem(line, 2) * 128, 128), 128), :] * product).astype(bf16)
             update[part * 32 + line] = result[:64]
             update[part * 32 + line + 16] = result[64:]
             return 0
 
-        lax.fori_loop(0, 16, finish, 0, unroll=8)
+        for begin in (0, 8):
+            lax.fori_loop(begin, begin + 8, finish, 0, unroll=8)
+            for base in (begin, begin + 16):
+                span = pl.ds(part * 32 + base, 8)
+                stores.append(pltpu.make_async_copy(update.at[span], update_hbm.at[span], store_sem.at[len(stores)]))
+                stores[-1].start()
 
     @pl.when(half == core)
     def _():
@@ -272,22 +310,24 @@
             pltpu.make_async_copy(span, span, send_sem.at[4 + part]).wait()
 
     handed.wait_send()
+    for store in stores:
+        store.wait()
 
 
 def local(rows, cols, pair, projection, out_weight):
     hidden = out_weight.shape[0]
     half_rows = rows // 2
-    vmem = pl.BlockSpec(memory_space=pltpu.VMEM)
     length = cols * 64
     return pl.pallas_call(
         functools.partial(kernel, rows, cols, hidden),
         out_shape=jax.ShapeDtypeStruct(pair.shape, bf16),
         in_specs=[pl.BlockSpec(memory_space=pltpu.HBM)] * 3,
-        out_specs=vmem,
+        out_specs=pl.BlockSpec(memory_space=pltpu.HBM),
         scratch_shapes=[
             pltpu.VMEM(pair.shape, bf16),
             pltpu.VMEM(projection.shape, bf16),
             pltpu.VMEM(out_weight.shape, bf16),
+            pltpu.VMEM(pair.shape, bf16),
             pltpu.VMEM((hidden * 32, 128), f32),
             pltpu.VMEM((hidden * 32, 128), f32),
             pltpu.VMEM((16, 256, 128), bf16),
@@ -304,6 +344,7 @@
             pltpu.VMEM((2, hidden, 16, 128), bf16),
             pltpu.VMEM((hidden * 16, 128), f32),
             pltpu.SemaphoreType.DMA((4,)),
+            pltpu.SemaphoreType.DMA((8,)),
             pltpu.SemaphoreType.REGULAR,
             pltpu.SemaphoreType.DMA((6,)),
             pltpu.SemaphoreType.DMA,
@@ -312,7 +353,7 @@
             pltpu.SemaphoreType.DMA((2,)),
         ],
         compiler_params=pltpu.CompilerParams(
-            collective_id=0, has_side_effects=True, vmem_limit_bytes=48 * 2**20
+            collective_id=0, has_side_effects=True, vmem_limit_bytes=58 * 2**20
         ),
         name="triangle",
     )(pair, projection, out_weight)

time: 94.3 us -> 87.5 us (0.928)
  Pallas kernels: 90.2 us -> 85.1 us
  local copies, waits for them, and re-layouts: 3.87 us -> 2.26 us
    pallas_call x1, Pallas kernels: 90.2 us -> 85.1 us  [local(): pl.pallas_call(functools.partial(kernel, rows, cols, hidden), out_shape=j...]
    unnamed x7 -> x1, local copies, waits for them, and re-layouts: 3.87 us -> 2.26 us
where the time goes in v3:
time: 87.5 us; the launch traced here: 87.4 us
  Pallas kernels  85.1 us (97%)
  local copies, waits for them, and re-layouts  2.26 us (3%)
    pallas_call x1, Pallas kernels, local(): pl.pallas_call(functools.partial(kernel, rows, cols, hidden), out_shape=j...  85.1 us
    unnamed x1, local copies, waits for them, and re-layouts  2.26 us

profile of v3, /device:TPU:1, one launch (start us, length us, event | category | flops | bytes accessed | tf_op | source)
XLA Modules:
  0.0 87.4 jit_solution(9835864655126865355)
XLA Ops:
  0.0 85.1 %triangle.1 = bf16[64,64,128]{2,1,0:T(8,128)(2,1)} custom-call(bf16[64,64,128]{2,1,0:T(8,128)(2,1)} %pair_hbm.1, bf16[128,640]{1,0:T(8,128)(2,1)} %projection_hbm.1, bf16[128,128]{1,0:T(8,128)(2,1)} %out_weight_hbm.1), custom_call_target="tpu_custom_call" | custom-call | tf_op jit(solution)/shard_map/triangle/pallas_call | solution.py:321
  85.1 2.3 %copy.5 = bf16[64,64,128]{2,1,0:T(8,128)(2,1)} copy(bf16[64,64,128]{2,1,0:T(8,128)(2,1)} %triangle.1) | data formatting | bytes 2097152

commit v4 on v3

--- a/solution.py
+++ b/solution.py
@@ -29,10 +29,10 @@
 
 def kernel(
     rows, cols, hidden,
-    pair_hbm, projection_hbm, out_weight_hbm, update_hbm,
-    pair, projection, out_weight, update, right_f32, left_f32, normed, gate, weights, right_send, left_send, right_got, left_got,
+    pair_hbm, projection_hbm, out_weight_hbm, update,
+    pair, projection, out_weight, right_f32, left_f32, normed, gate, weights, right_send, left_send, right_got, left_got,
     right_all, left_all, mixed, mixed_send, mixed_got, mixed_f32,
-    load_sem, store_sem, entered_sem, send_sem, right_sem, left_sem, twin_sem, mixed_sem,
+    load_sem, entered_sem, send_sem, right_sem, left_sem, twin_sem, mixed_sem,
 ):
     chips = rows * cols // 2
     half_rows = rows // 2
@@ -255,7 +255,6 @@
             mixed_message(place, col).start()
 
     loads[3].wait()
-    stores = []
     for part in range(2):
         pltpu.make_async_copy(mixed_got.at[part], mixed_got.at[part], mixed_sem.at[part]).wait()
 
@@ -284,12 +283,7 @@
             update[part * 32 + line + 16] = result[64:]
             return 0
 
-        for begin in (0, 8):
-            lax.fori_loop(begin, begin + 8, finish, 0, unroll=8)
-            for base in (begin, begin + 16):
-                span = pl.ds(part * 32 + base, 8)
-                stores.append(pltpu.make_async_copy(update.at[span], update_hbm.at[span], store_sem.at[len(stores)]))
-                stores[-1].start()
+        lax.fori_loop(0, 16, finish, 0, unroll=8)
 
     @pl.when(half == core)
     def _():
@@ -310,24 +304,22 @@
             pltpu.make_async_copy(span, span, send_sem.at[4 + part]).wait()
 
     handed.wait_send()
-    for store in stores:
-        store.wait()
 
 
 def local(rows, cols, pair, projection, out_weight):
     hidden = out_weight.shape[0]
     half_rows = rows // 2
+    vmem = pl.BlockSpec(memory_space=pltpu.VMEM)
     length = cols * 64
     return pl.pallas_call(
         functools.partial(kernel, rows, cols, hidden),
         out_shape=jax.ShapeDtypeStruct(pair.shape, bf16),
         in_specs=[pl.BlockSpec(memory_space=pltpu.HBM)] * 3,
-        out_specs=pl.BlockSpec(memory_space=pltpu.HBM),
+        out_specs=vmem,
         scratch_shapes=[
             pltpu.VMEM(pair.shape, bf16),
             pltpu.VMEM(projection.shape, bf16),
             pltpu.VMEM(out_weight.shape, bf16),
-            pltpu.VMEM(pair.shape, bf16),
             pltpu.VMEM((hidden * 32, 128), f32),
             pltpu.VMEM((hidden * 32, 128), f32),
             pltpu.VMEM((16, 256, 128), bf16),
@@ -344,7 +336,6 @@
             pltpu.VMEM((2, hidden, 16, 128), bf16),
             pltpu.VMEM((hidden * 16, 128), f32),
             pltpu.SemaphoreType.DMA((4,)),
-            pltpu.SemaphoreType.DMA((8,)),
             pltpu.SemaphoreType.REGULAR,
             pltpu.SemaphoreType.DMA((6,)),
             pltpu.SemaphoreType.DMA,
@@ -353,10 +344,10 @@
             pltpu.SemaphoreType.DMA((2,)),
         ],
         compiler_params=pltpu.CompilerParams(
-            collective_id=0, has_side_effects=True, vmem_limit_bytes=58 * 2**20
+            collective_id=0, has_side_effects=True, vmem_limit_bytes=48 * 2**20
         ),
         name="triangle",
-    )(pair, projection, out_weight)
+    )(*[pltpu.with_memory_space_constraint(x, pltpu.HBM) for x in (pair, projection, out_weight)])
 
 
 def solution(mesh):

time: 87.5 us -> 85.6 us (0.978)
  local copies, waits for them, and re-layouts: 2.26 us -> 0.97 us
    unnamed x1, local copies, waits for them, and re-layouts: 2.26 us -> 0.97 us
where the time goes in v4:
time: 85.6 us; the launch traced here: 85.5 us
  Pallas kernels  84.5 us (99%)
  local copies, waits for them, and re-layouts  0.97 us (1%)
    pallas_call x1, Pallas kernels, local(): pl.pallas_call(functools.partial(kernel, rows, cols, hidden), out_shape=j...  84.5 us

profile of v4, /device:TPU:1, one launch (start us, length us, event | category | flops | bytes accessed | tf_op | source)
XLA Modules:
  0.0 85.5 jit_solution(3354732912806754344)
XLA Ops:
  0.0 84.5 %triangle.1 = bf16[64,64,128]{2,1,0:T(8,128)(2,1)S(1)} custom-call(bf16[64,64,128]{2,1,0:T(8,128)(2,1)} %pair_hbm.1, bf16[128,640]{1,0:T(8,128)(2,1)} %projection_hbm.1, bf16[128,128]{1,0:T(8,128)(2,1)} %out_weight_hbm.1), custom_call_target="tpu_custom_call" | custom-call | tf_op jit(solution)/shard_map/triangle/pallas_call | solution.py:314
  84.5 1.0 %copy.5 = bf16[64,64,128]{2,1,0:T(8,128)(2,1)} copy(bf16[64,64,128]{2,1,0:T(8,128)(2,1)S(1)} %triangle.1) | data formatting | bytes 2097152

commit v5 on v4

--- a/solution.py
+++ b/solution.py
@@ -48,8 +48,8 @@
     def chip(x, y, z):
         return y * 4 + z // 2, x * 2 + rem(z, 2)
 
-    def along_z(k):
-        return rem(z + 4 + ((k + 1) // 2) * (1 - 2 * rem(k, 2)) + lines_z, lines_z)
+    def other(place, k, count):
+        return rem(place + count // 2 + ((k + 1) // 2) * (1 - 2 * rem(k, 2)) + count, count)
 
     loads = [
         pltpu.make_async_copy(projection_hbm, projection, load_sem.at[0]),
@@ -60,12 +60,13 @@
     for load in loads:
         load.start()
 
+    near = planes * lines_z
     barrier = pltpu.get_barrier_semaphore()
     x_peers = [(row, rem(col + 4 * step, cols)) for step in range(1, columns)]
     for k in range(lines_z):
         for step in range(planes):
-            place, pair_place = chip(x, rem(y + step, planes), along_z(k))
-            if k < lines_z - 1 or step > 0:
+            place, pair_place = chip(x, other(y, step, planes), other(z, k, lines_z))
+            if k < lines_z - 1 or step < planes - 1:
                 pl.semaphore_signal(barrier, inc=1, device_id=(place, pair_place * 2), device_id_type=MESH)
                 pl.semaphore_signal(barrier, inc=1, device_id=(place, pair_place * 2 + 1), device_id_type=MESH)
     for peer in [twin] + x_peers:
@@ -96,22 +97,18 @@
         right_f32[pl.ds(2 * step + 1, hidden, stride=32), :] = side[:, 128:]
         return 0
 
-    for part in range(2):
-        loads[1 + part].wait()
-        lax.fori_loop(8 * part, 8 * part + 8, norm, 0, unroll=2)
-    lax.fori_loop(0, 16, right_side, 0, unroll=4)
-
-    def send_side(held, outgoing, got, sem, sent, first, size, start, stop):
+    def send_side(held, outgoing, got, sem, sent, first, stop, apart_too, with_own):
         def fill(channel):
             base = pl.multiple_of(channel * 32 + first, 16)
-            outgoing[channel, first : first + size] = held[pl.ds(base, size), :].astype(bf16)
-            return outgoing.at[channel, pl.ds(first, size)]
+            outgoing[channel, first : first + 16] = held[pl.ds(base, 16), :].astype(bf16)
+            return outgoing.at[channel, pl.ds(first, 16)]
 
         def body(step, _):
+            apart = step // near
             place, pair_place = chip(
-                rem(x + step // (planes * lines_z), columns),
-                rem(y + step // lines_z + 1, planes),
-                along_z(rem(step, lines_z)),
+                other(x, apart, columns) if apart_too else x,
+                other(y, rem(step // lines_z, planes), planes),
+                other(z, rem(step, lines_z), lines_z),
             )
             pltpu.make_async_remote_copy(
                 src_ref=fill(place * (cols // 2) + pair_place), dst_ref=got, send_sem=sent, recv_sem=sem,
@@ -119,12 +116,11 @@
             ).start()
             return 0
 
-        own = planes * lines_z - 1
-        if start <= own:
-            head = (own - start) % 4
-            for step in range(start, start + head):
-                body(step, 0)
-            lax.fori_loop(start + head, own, body, 0, unroll=4)
+        own = stop - 1 if with_own else stop
+        for step in range(0, own % 4):
+            body(step, 0)
+        lax.fori_loop(own % 4, own, body, 0, unroll=4)
+        if with_own:
             source = fill(mine)
 
             @pl.when(half == core)
@@ -137,17 +133,22 @@
                     src_ref=source, dst_ref=got, send_sem=sent, recv_sem=sem, device_id=twin, device_id_type=MESH
                 ).start()
 
-            start = own + 1
-        lax.fori_loop(start, stop, body, 0, unroll=4)
-
-    right_slot = right_got.at[half, col, slot_row]
-    near = planes * lines_z
-    pl.semaphore_wait(barrier, 2 * near - 1 + columns - 1)
-    for peer in x_peers:
-        pl.semaphore_signal(entered_sem, inc=1, device_id=peer, device_id_type=MESH)
-    send_side(right_f32, right_send, right_slot, right_sem, send_sem.at[0], 0, 32, 0, near)
+    def send_right(part, stop, apart_too, with_own):
+        got = right_got.at[half, col, slot_row, pl.ds(16 * part, 16)]
+        send_side(right_f32, right_send, got, right_sem, send_sem.at[0], 16 * part, stop, apart_too, with_own)
+
+    for part in range(2):
+        loads[1 + part].wait()
+        lax.fori_loop(8 * part, 8 * part + 8, norm, 0, unroll=2)
+        lax.fori_loop(8 * part, 8 * part + 8, right_side, 0, unroll=4)
+        if part == 0:
+            pl.semaphore_wait(barrier, 2 * near - 1 + columns - 1)
+            for peer in x_peers:
+                pl.semaphore_signal(entered_sem, inc=1, device_id=peer, device_id_type=MESH)
+        send_right(part, near, False, True)
     pl.semaphore_wait(entered_sem, columns - 1)
-    send_side(right_f32, right_send, right_slot, right_sem, send_sem.at[0], 0, 32, near, chips)
+    for part in range(2):
+        send_right(part, chips - near, True, False)
 
     def left_side(step, _):
         both = dot(weights[: 2 * hidden], normed[step], ((1,), (1,)))
@@ -160,7 +161,7 @@
         lax.fori_loop(8 * part, 8 * part + 8, left_side, 0, unroll=4)
         send_side(
             left_f32, left_send, left_got.at[part, col, slot_row], left_sem.at[part], send_sem.at[1 + part],
-            16 * part, 16, 0, chips,
+            16 * part, chips, True, True,
         )
 
     def gate_of(step, _):
@@ -223,20 +224,19 @@
 
         got = mixed_got.at[part, mine]
 
-        def mixed_message(place, other):
+        def mixed_message(place, to):
             line = rem(place, half_rows)
             return pltpu.make_async_remote_copy(
-                src_ref=mixed_send.at[part, line, other], dst_ref=got,
+                src_ref=mixed_send.at[part, line, to], dst_ref=got,
                 send_sem=send_sem.at[4 + part], recv_sem=mixed_sem.at[part],
-                device_id=(place, other), device_id_type=MESH,
+                device_id=(place, to), device_id_type=MESH,
             )
 
         def send_mixed(step, _):
-            k = rem(step, lines_z)
-            other_core = rem(core + 1 + step // lines_z, 2)
-            other_y = core * (planes // 2) + rem(y + 1 + step // (2 * lines_z), planes // 2)
-            other_x = rem(x + 1 + step // (planes * lines_z), columns)
-            place, pair_place = chip(other_x, other_y, along_z(k))
+            other_core = other(core, rem(step // lines_z, 2), 2)
+            other_y = core * (planes // 2) + other(rem(y, planes // 2), rem(step // (2 * lines_z), planes // 2), planes // 2)
+            other_x = other(x, step // near, columns)
+            place, pair_place = chip(other_x, other_y, other(z, rem(step, lines_z), lines_z))
             mixed_message(place, pair_place * 2 + other_core).start()
             return 0
 

time: 85.6 us -> 84.2 us (0.984)
  Pallas kernels: 84.5 us -> 83.1 us
    pallas_call x1, Pallas kernels: 84.5 us -> 83.1 us  [local(): pl.pallas_call(functools.partial(kernel, rows, cols, hidden), out_shape=j...]
where the time goes in v5:
time: 84.2 us; the launch traced here: 84.1 us
  Pallas kernels  83.1 us (99%)
  local copies, waits for them, and re-layouts  0.97 us (1%)
    pallas_call x1, Pallas kernels, local(): pl.pallas_call(functools.partial(kernel, rows, cols, hidden), out_shape=j...  83.1 us

profile of v5, /device:TPU:1, one launch (start us, length us, event | category | flops | bytes accessed | tf_op | source)
XLA Modules:
  0.0 84.1 jit_solution(944917660127569628)
XLA Ops:
  0.0 83.1 %triangle.1 = bf16[64,64,128]{2,1,0:T(8,128)(2,1)S(1)} custom-call(bf16[64,64,128]{2,1,0:T(8,128)(2,1)} %pair_hbm.1, bf16[128,640]{1,0:T(8,128)(2,1)} %projection_hbm.1, bf16[128,128]{1,0:T(8,128)(2,1)} %out_weight_hbm.1), custom_call_target="tpu_custom_call" | custom-call | tf_op jit(solution)/shard_map/triangle/pallas_call | solution.py:314
  83.1 1.0 %copy.5 = bf16[64,64,128]{2,1,0:T(8,128)(2,1)} copy(bf16[64,64,128]{2,1,0:T(8,128)(2,1)S(1)} %triangle.1) | data formatting | bytes 2097152

commit v6 on v5

--- a/solution.py
+++ b/solution.py
@@ -64,13 +64,23 @@
     barrier = pltpu.get_barrier_semaphore()
     x_peers = [(row, rem(col + 4 * step, cols)) for step in range(1, columns)]
     for k in range(lines_z):
-        for step in range(planes):
-            place, pair_place = chip(x, other(y, step, planes), other(z, k, lines_z))
-            if k < lines_z - 1 or step < planes - 1:
-                pl.semaphore_signal(barrier, inc=1, device_id=(place, pair_place * 2), device_id_type=MESH)
-                pl.semaphore_signal(barrier, inc=1, device_id=(place, pair_place * 2 + 1), device_id_type=MESH)
+        for step in range(planes // 2):
+            other_y = core * (planes // 2) + other(rem(y, planes // 2), step, planes // 2)
+            place, pair_place = chip(x, other_y, other(z, k, lines_z))
+            peers = [(place, pair_place * 2 + 1 - core), (place, pair_place * 2 + core)]
+            if k < lines_z - 1 or step < planes // 2 - 1:
+                for peer in peers:
+                    pl.semaphore_signal(barrier, inc=1, device_id=peer, device_id_type=MESH)
+            else:
+                pl.semaphore_signal(barrier, inc=1, device_id=peers[0], device_id_type=MESH)
+
+                @pl.when(half != core)
+                def _():
+                    pl.semaphore_signal(barrier, inc=1, device_id=peers[1], device_id_type=MESH)
+
     for peer in [twin] + x_peers:
         pl.semaphore_signal(barrier, inc=1, device_id=peer, device_id_type=MESH)
+    expected = near + columns - jnp.where(half == core, 1, 0)
 
     loads[0].wait()
     weights[...] = projection[:, : 4 * hidden].T
@@ -142,7 +152,7 @@
         lax.fori_loop(8 * part, 8 * part + 8, norm, 0, unroll=2)
         lax.fori_loop(8 * part, 8 * part + 8, right_side, 0, unroll=4)
         if part == 0:
-            pl.semaphore_wait(barrier, 2 * near - 1 + columns - 1)
+            pl.semaphore_wait(barrier, expected)
             for peer in x_peers:
                 pl.semaphore_signal(entered_sem, inc=1, device_id=peer, device_id_type=MESH)
         send_right(part, near, False, True)
@@ -259,20 +269,20 @@
         pltpu.make_async_copy(mixed_got.at[part], mixed_got.at[part], mixed_sem.at[part]).wait()
 
         total = jnp.zeros((16, 128), f32)
-        total = lax.fori_loop(0, hidden, lambda c, t: t + mixed_got[part, c].astype(f32), total, unroll=min(16, hidden))
+        total = lax.fori_loop(0, hidden, lambda c, t: t + mixed_got[part, c].astype(f32), total, unroll=min(32, hidden))
         mean = total * (1.0 / hidden)
 
         def square(c, t):
             centered = mixed_got[part, c].astype(f32) - mean
             return t + centered * centered
 
-        scale = lax.rsqrt(lax.fori_loop(0, hidden, square, jnp.zeros((16, 128), f32), unroll=min(16, hidden)) * (1.0 / hidden) + epsilon)
+        scale = lax.rsqrt(lax.fori_loop(0, hidden, square, jnp.zeros((16, 128), f32), unroll=min(32, hidden)) * (1.0 / hidden) + epsilon)
 
         def scaled(c, _):
             mixed_f32[pl.ds(pl.multiple_of(c * 16, 16), 16), :] = (mixed_got[part, c].astype(f32) - mean) * scale
             return 0
 
-        lax.fori_loop(0, hidden, scaled, 0, unroll=min(16, hidden))
+        lax.fori_loop(0, hidden, scaled, 0, unroll=min(32, hidden))
 
         def finish(line, _):
             unit = mixed_f32[pl.ds(line, hidden, stride=16), :].astype(bf16)
@@ -283,7 +293,7 @@
             update[part * 32 + line + 16] = result[64:]
             return 0
 
-        lax.fori_loop(0, 16, finish, 0, unroll=8)
+        lax.fori_loop(0, 16, finish, 0, unroll=16)
 
     @pl.when(half == core)
     def _():

time: 84.2 us -> 83.6 us (level)
  no operation moved by 1% of the time
where the time goes in v6:
time: 83.6 us; the launch traced here: 83.5 us
  Pallas kernels  82.5 us (99%)
  local copies, waits for them, and re-layouts  0.97 us (1%)
    pallas_call x1, Pallas kernels, local(): pl.pallas_call(functools.partial(kernel, rows, cols, hidden), out_shape=j...  82.5 us

profile of v6, /device:TPU:1, one launch (start us, length us, event | category | flops | bytes accessed | tf_op | source)
XLA Modules:
  0.0 83.5 jit_solution(8808623745649034575)
XLA Ops:
  0.0 82.5 %triangle.1 = bf16[64,64,128]{2,1,0:T(8,128)(2,1)S(1)} custom-call(bf16[64,64,128]{2,1,0:T(8,128)(2,1)} %pair_hbm.1, bf16[128,640]{1,0:T(8,128)(2,1)} %projection_hbm.1, bf16[128,128]{1,0:T(8,128)(2,1)} %out_weight_hbm.1), custom_call_target="tpu_custom_call" | custom-call | tf_op jit(solution)/shard_map/triangle/pallas_call | solution.py:324
  82.5 1.0 %copy.5 = bf16[64,64,128]{2,1,0:T(8,128)(2,1)} copy(bf16[64,64,128]{2,1,0:T(8,128)(2,1)S(1)} %triangle.1) | data formatting | bytes 2097152

commit v7 on v6

--- a/solution.py
+++ b/solution.py
@@ -57,8 +57,8 @@
         pltpu.make_async_copy(pair_hbm.at[pl.ds(32, 32)], pair.at[pl.ds(32, 32)], load_sem.at[2]),
         pltpu.make_async_copy(out_weight_hbm, out_weight, load_sem.at[3]),
     ]
-    for load in loads:
-        load.start()
+    for order in (1, 0, 2, 3):
+        loads[order].start()
 
     near = planes * lines_z
     barrier = pltpu.get_barrier_semaphore()
@@ -82,9 +82,6 @@
         pl.semaphore_signal(barrier, inc=1, device_id=peer, device_id_type=MESH)
     expected = near + columns - jnp.where(half == core, 1, 0)
 
-    loads[0].wait()
-    weights[...] = projection[:, : 4 * hidden].T
-
     def lines(step):
         block, inner = step // 8, rem(step, 8) * 2
         return block * 32 + inner
@@ -150,6 +147,9 @@
     for part in range(2):
         loads[1 + part].wait()
         lax.fori_loop(8 * part, 8 * part + 8, norm, 0, unroll=2)
+        if part == 0:
+            loads[0].wait()
+            weights[...] = projection[:, : 4 * hidden].T
         lax.fori_loop(8 * part, 8 * part + 8, right_side, 0, unroll=4)
         if part == 0:
             pl.semaphore_wait(barrier, expected)
@@ -330,8 +330,8 @@
             pltpu.VMEM(pair.shape, bf16),
             pltpu.VMEM(projection.shape, bf16),
             pltpu.VMEM(out_weight.shape, bf16),
-            pltpu.VMEM((hidden * 32, 128), f32),
-            pltpu.VMEM((hidden * 32, 128), f32),
+            pltpu.VMEM((hidden * 32 + 32, 128), f32),
+            pltpu.VMEM((hidden * 32 + 32, 128), f32),
             pltpu.VMEM((16, 256, 128), bf16),
             pltpu.VMEM((16, 256, 128), f32),
             pltpu.VMEM((4 * hidden, 128), bf16),
@@ -344,7 +344,7 @@
             pltpu.VMEM((half_rows * 32, 256), bf16),
             pltpu.VMEM((2, half_rows, cols, 16, 128), bf16),
             pltpu.VMEM((2, hidden, 16, 128), bf16),
-            pltpu.VMEM((hidden * 16, 128), f32),
+            pltpu.VMEM((hidden * 16 + 16, 128), f32),
             pltpu.SemaphoreType.DMA((4,)),
             pltpu.SemaphoreType.REGULAR,
             pltpu.SemaphoreType.DMA((6,)),

time: 83.6 us -> 83.6 us (level)
  no operation moved by 1% of the time
where the time goes in v7:
time: 83.6 us; the launch traced here: 83.5 us
  Pallas kernels  82.5 us (99%)
  local copies, waits for them, and re-layouts  0.97 us (1%)
    pallas_call x1, Pallas kernels, local(): pl.pallas_call(functools.partial(kernel, rows, cols, hidden), out_shape=j...  82.5 us

profile of v7, /device:TPU:1, one launch (start us, length us, event | category | flops | bytes accessed | tf_op | source)
XLA Modules:
  0.0 83.5 jit_solution(38839370453198234)
XLA Ops:
  0.0 82.5 %triangle.1 = bf16[64,64,128]{2,1,0:T(8,128)(2,1)S(1)} custom-call(bf16[64,64,128]{2,1,0:T(8,128)(2,1)} %pair_hbm.1, bf16[128,640]{1,0:T(8,128)(2,1)} %projection_hbm.1, bf16[128,128]{1,0:T(8,128)(2,1)} %out_weight_hbm.1), custom_call_target="tpu_custom_call" | custom-call | tf_op jit(solution)/shard_map/triangle/pallas_call | solution.py:324
  82.5 1.0 %copy.5 = bf16[64,64,128]{2,1,0:T(8,128)(2,1)} copy(bf16[64,64,128]{2,1,0:T(8,128)(2,1)S(1)} %triangle.1) | data formatting | bytes 2097152

commit v8 on v7

--- a/solution.py
+++ b/solution.py
@@ -268,15 +268,20 @@
     for part in range(2):
         pltpu.make_async_copy(mixed_got.at[part], mixed_got.at[part], mixed_sem.at[part]).wait()
 
-        total = jnp.zeros((16, 128), f32)
-        total = lax.fori_loop(0, hidden, lambda c, t: t + mixed_got[part, c].astype(f32), total, unroll=min(32, hidden))
-        mean = total * (1.0 / hidden)
-
-        def square(c, t):
+        def sum_of(term):
+            zero = jnp.zeros((16, 128), f32)
+            sums = lax.fori_loop(
+                0, hidden // 4, lambda c, t: tuple(t[n] + term(4 * c + n) for n in range(4)), (zero,) * 4, unroll=8
+            )
+            return (sums[0] + sums[1]) + (sums[2] + sums[3])
+
+        mean = sum_of(lambda c: mixed_got[part, c].astype(f32)) * (1.0 / hidden)
+
+        def square(c):
             centered = mixed_got[part, c].astype(f32) - mean
-            return t + centered * centered
-
-        scale = lax.rsqrt(lax.fori_loop(0, hidden, square, jnp.zeros((16, 128), f32), unroll=min(32, hidden)) * (1.0 / hidden) + epsilon)
+            return centered * centered
+
+        scale = lax.rsqrt(sum_of(square) * (1.0 / hidden) + epsilon)
 
         def scaled(c, _):
             mixed_f32[pl.ds(pl.multiple_of(c * 16, 16), 16), :] = (mixed_got[part, c].astype(f32) - mean) * scale

time: 83.6 us -> 83.5 us (level)
  no operation moved by 1% of the time
where the time goes in v8:
time: 83.5 us; the launch traced here: 83.4 us
  Pallas kernels  82.4 us (99%)
  local copies, waits for them, and re-layouts  0.97 us (1%)
    pallas_call x1, Pallas kernels, local(): pl.pallas_call(functools.partial(kernel, rows, cols, hidden), out_shape=j...  82.4 us

profile of v8, /device:TPU:1, one launch (start us, length us, event | category | flops | bytes accessed | tf_op | source)
XLA Modules:
  0.0 83.4 jit_solution(10267485788718050260)
XLA Ops:
  0.0 82.4 %triangle.1 = bf16[64,64,128]{2,1,0:T(8,128)(2,1)S(1)} custom-call(bf16[64,64,128]{2,1,0:T(8,128)(2,1)} %pair_hbm.1, bf16[128,640]{1,0:T(8,128)(2,1)} %projection_hbm.1, bf16[128,128]{1,0:T(8,128)(2,1)} %out_weight_hbm.1), custom_call_target="tpu_custom_call" | custom-call | tf_op jit(solution)/shard_map/triangle/pallas_call | solution.py:329
  82.4 1.0 %copy.5 = bf16[64,64,128]{2,1,0:T(8,128)(2,1)} copy(bf16[64,64,128]{2,1,0:T(8,128)(2,1)S(1)} %triangle.1) | data formatting | bytes 2097152
